TPU v7x, 32 devices: a whole 2x2x4 slice. The times are simulated.
32 devices in a mesh: scale: 4 (over x, core), space: 8 (over z, y).
Axes of the slice: x: 2, y: 2, z: 4, core: 2. Of those that a mesh axis runs over, the one named last changes fastest.
Arguments:
- features: bfloat16 [4, 32, 128, 512], P('scale', 'space'), may hold values from -6 to 6
- valid_rows: int32 [4], replicated, may hold values from 8 to 32, as said below
- conv_master: float32 [3, 4608, 512], P(None, 'space'), may hold values from -0.125 to 0.125
- head_master: float32 [917504], P(('scale', 'space')), may hold values from -0.25 to 0.25
- vectors: float32 [5120], replicated
- conv_first: float32 [3, 4608, 512], P(None, 'space'), may hold values from -40 to 40
- conv_second: float32 [3, 4608, 512], P(None, 'space'), may hold values from 186.14845 to 744.5938
- head_first: float32 [917504], P(('scale', 'space')), may hold values from -40 to 40
- head_second: float32 [917504], P(('scale', 'space')), may hold values from 186.14845 to 744.5938
- vec_first: float32 [5120], replicated
- vec_second: float32 [5120], replicated
- statistics: float32 [3, 512, 512], replicated, as said below
- bases: float32 [3, 512, 512], replicated, as said below
- cotangent: bfloat16 [32, 128, 1792], P('space'), may hold values from -6 to 6
Outputs:
- merged: bfloat16 [32, 128, 1792], P('space')
- features_grad: bfloat16 [4, 32, 128, 512], P('scale', 'space')
- conv_first_new: float32 [3, 4608, 512], P(None, 'space')
- conv_second_new: float32 [3, 4608, 512], P(None, 'space')
- conv_new: float32 [3, 4608, 512], P(None, 'space')
- head_first_new: float32 [917504], P(('scale', 'space'))
- head_second_new: float32 [917504], P(('scale', 'space'))
- head_new: float32 [917504], P(('scale', 'space'))
- vec_first_new: float32 [5120], replicated
- vec_second_new: float32 [5120], replicated
- vec_new: float32 [5120], replicated
- statistics_new: float32 [3, 512, 512], replicated
- bases_new: float32 [3, 512, 512], replicated
Inputs may be any that keep to these rules, and one draw needn't show every extreme that they name: `valid_rows`: one scale, drawn from the seed, fills all 32 rows. `statistics`: each matrix is symmetric positive definite. `bases`: each matrix is orthogonal.
All inputs are finite; a program needn't handle non-finite values.
Results may differ from a plain program's by a relative error of at most 0.014.
Values may be sent and summed in bfloat16 or wider, within the bound.
A program may use at most 256 MiB of HBM per device.

v0:
```python
import jax
import jax.numpy as jnp
from jax import lax
from jax.sharding import PartitionSpec as P

NH = 7
HD = 256
STEP = 5


BETA_ONE = 0.9
BETA_TWO = 0.95
EPSILON = 1e-08
DECAY = 0.01
RATE_CONV = 0.04
RATE_HEAD = 0.08
RATE_BIAS = 0.5
RATE_GAIN = 20.0


def padded_2(block, sides, width):
    for axis, dim in sides:
        count = lax.axis_size(axis)
        forward = [(i, i + 1) for i in range(count - 1)]
        backward = [(target, source) for source, target in forward]
        low = lax.ppermute(
            lax.slice_in_dim(block, block.shape[dim] - width, None, axis=dim), axis, forward
        )
        high = lax.ppermute(lax.slice_in_dim(block, 0, width, axis=dim), axis, backward)
        block = jnp.concatenate([low, block, high], axis=dim)
    return block


def widen(rows_in):
    return jnp.pad(rows_in, ((0, 0), (1, 1), (0, 0)))


def convolve_valid(padded, kernel):
    return lax.conv_general_dilated(
        padded[None],
        kernel,
        (1, 1),
        "VALID",
        dimension_numbers=("NHWC", "HWIO", "NHWC"),
        preferred_element_type=jnp.float32,
    )[0]


def moments(grads, first, second):
    first_new = BETA_ONE * first + (1.0 - BETA_ONE) * grads
    second_new = BETA_TWO * second + (1.0 - BETA_TWO) * grads * grads
    direction = (
        first_new
        / (1.0 - BETA_ONE**STEP)
        / (jnp.sqrt(second_new / (1.0 - BETA_TWO**STEP)) + EPSILON)
    )
    return (first_new, second_new, direction)


def renew(stats_new, bases):
    product = jnp.einsum("lcd,lde->lce", stats_new, bases, precision=lax.Precision.HIGHEST)
    gram = jnp.einsum("lce,lcf->lef", product, product, precision=lax.Precision.HIGHEST)
    lower = jnp.linalg.cholesky(gram)
    solved = jax.vmap(
        lambda factor, matrix: jax.scipy.linalg.solve_triangular(factor, matrix.T, lower=True)
    )(lower, product)
    return jnp.transpose(solved, (0, 2, 1))


def local(
    features,
    valid_rows,
    conv_master,
    head_master,
    vectors,
    conv_first,
    conv_second,
    head_first,
    head_second,
    vec_first,
    vec_second,
    statistics,
    bases,
    cotangent,
):
    channels = features.shape[3]
    rows_dev = features.shape[1]
    width = features.shape[2]
    head_width = cotangent.shape[2]
    conv_used = lax.all_gather(conv_master.astype(jnp.bfloat16), "space", axis=1, tiled=True)
    head_flat = lax.all_gather(
        head_master.astype(jnp.bfloat16), ("scale", "space"), axis=0, tiled=True
    )
    head_used = head_flat.reshape(channels, head_width)
    conv_bias = vectors[: 3 * channels].reshape(3, channels)
    head_bias = vectors[3 * channels : 3 * channels + head_width]
    head_gain = vectors[3 * channels + head_width :]
    row_index = lax.axis_index("space") * rows_dev + jnp.arange(rows_dev, dtype=jnp.int32)
    row_mask = (row_index < valid_rows[lax.axis_index("scale")]).astype(jnp.float32)
    counts = jnp.sum((row_index[None, :] < valid_rows[:, None]).astype(jnp.float32), 0)
    mask_cube = row_mask[:, None, None]
    inputs = features[0]
    kept_hidden = []
    kept_inputs = []
    kernels = []
    for which_layer in range(3):
        padded = widen(padded_2(inputs, (("space", 0),), 1))
        kernel = conv_used[which_layer].reshape(3, 3, channels, channels)
        hidden = convolve_valid(padded, kernel) + conv_bias[which_layer]
        kept_hidden.append(hidden)
        kernels.append(kernel)
        kept_inputs.append(padded)
        inputs = (jax.nn.gelu(hidden) * mask_cube).astype(jnp.bfloat16)
    flattened = inputs.reshape(rows_dev * width, channels)
    projected = jnp.dot(flattened, head_used, preferred_element_type=jnp.float32) + head_bias
    per_head = projected.reshape(-1, NH, HD)
    inverse = lax.rsqrt(jnp.sum(per_head * per_head, -1, keepdims=True) + 1e-06)
    normed_head = per_head * inverse
    normed = normed_head.reshape(-1, head_width)
    weights_row = (row_mask / counts)[:, None, None]
    term = (normed * head_gain).reshape(rows_dev, width, head_width) * weights_row
    merged = lax.psum(term.astype(jnp.bfloat16), "scale")
    d_out = (cotangent.astype(jnp.float32) * weights_row).reshape(-1, head_width)
    grad_gain = jnp.sum(normed * d_out, 0)
    d_normed = (d_out * head_gain).reshape(-1, NH, HD)
    d_proj = inverse * (d_normed - normed_head * jnp.sum(normed_head * d_normed, -1, keepdims=True))
    d_low = d_proj.reshape(-1, head_width).astype(jnp.bfloat16)
    grad_head_bias = jnp.sum(d_low.astype(jnp.float32), 0)
    grad_head = jnp.einsum("pc,pf->cf", flattened, d_low, preferred_element_type=jnp.float32)
    d_active = jnp.einsum(
        "pf,cf->pc", d_low, head_used, preferred_element_type=jnp.float32
    ).reshape(rows_dev, width, channels)
    conv_grads = [None, None, None]
    bias_grads = [None, None, None]
    for which_layer in (2, 1, 0):
        unused, gelu_pull = jax.vjp(jax.nn.gelu, kept_hidden[which_layer])
        d_hidden = gelu_pull(d_active * mask_cube)[0].astype(jnp.bfloat16)
        bias_grads[which_layer] = jnp.sum(d_hidden.astype(jnp.float32), (0, 1))
        padded_in = kept_inputs[which_layer]
        tap_grads = []
        for tap_row in range(3):
            for tap_col in range(3):
                window = padded_in[tap_row : tap_row + rows_dev, tap_col : tap_col + width, :]
                tap_grads.append(
                    jnp.einsum("rwi,rwo->io", window, d_hidden, preferred_element_type=jnp.float32)
                )
        conv_grads[which_layer] = jnp.stack(tap_grads).reshape(9 * channels, channels)
        d_padded = widen(padded_2(d_hidden, (("space", 0),), 1))
        flipped = jnp.transpose(jnp.flip(kernels[which_layer], (0, 1)), (0, 1, 3, 2))
        d_active = convolve_valid(d_padded, flipped)
    features_grad = d_active.astype(jnp.bfloat16)[None]
    stacked_grads = jnp.stack(conv_grads)
    conv_part = lax.psum_scatter(stacked_grads, "space", scatter_dimension=1, tiled=True)
    owned_conv = lax.psum(conv_part.astype(jnp.bfloat16), "scale").astype(jnp.float32)
    owned_head = lax.psum_scatter(
        grad_head.reshape(-1), ("scale", "space"), scatter_dimension=0, tiled=True
    )
    partial_stats = jnp.einsum(
        "lrc,lrd->lcd", owned_conv, owned_conv, precision=lax.Precision.HIGHEST
    ) / lax.axis_size("scale")
    vec_partial = jnp.concatenate([jnp.concatenate(bias_grads), grad_head_bias, grad_gain])
    summed_stats, grad_vec = lax.psum((partial_stats, vec_partial), ("scale", "space"))
    rotated = jnp.einsum("lrc,lcd->lrd", owned_conv, bases, precision=lax.Precision.HIGHEST)
    conv_first_new, conv_second_new, direction = moments(rotated, conv_first, conv_second)
    turned = jnp.einsum("lrd,lcd->lrc", direction, bases, precision=lax.Precision.HIGHEST)
    conv_new = conv_master - RATE_CONV * (turned + DECAY * conv_master)
    head_first_new, head_second_new, head_dir = moments(owned_head, head_first, head_second)
    head_new = head_master - RATE_HEAD * (head_dir + DECAY * head_master)
    vec_first_new, vec_second_new, vec_dir = moments(grad_vec, vec_first, vec_second)
    rates = jnp.concatenate(
        [
            jnp.full((3 * channels + head_width,), RATE_BIAS, jnp.float32),
            jnp.full((head_width,), RATE_GAIN, jnp.float32),
        ]
    )
    vec_new = vectors - rates * (vec_dir + DECAY * vectors)
    stats_new = BETA_TWO * statistics + (1.0 - BETA_TWO) * summed_stats
    bases_new = renew(stats_new, bases)
    return (
        merged,
        features_grad,
        conv_first_new,
        conv_second_new,
        conv_new,
        head_first_new,
        head_second_new,
        head_new,
        vec_first_new,
        vec_second_new,
        vec_new,
        stats_new,
        bases_new,
    )


def solution(mesh):
    in_specs = (
        P("scale", "space", None, None),
        P(),
        P(None, "space", None),
        P(("scale", "space")),
        P(),
        P(None, "space", None),
        P(None, "space", None),
        P(("scale", "space")),
        P(("scale", "space")),
        P(),
        P(),
        P(),
        P(),
        P("space", None, None),
    )
    out_specs = (
        P("space", None, None),
        P("scale", "space", None, None),
        P(None, "space", None),
        P(None, "space", None),
        P(None, "space", None),
        P(("scale", "space")),
        P(("scale", "space")),
        P(("scale", "space")),
        P(),
        P(),
        P(),
        P(),
        P(),
    )
    return jax.shard_map(local, mesh=mesh, in_specs=in_specs, out_specs=out_specs, check_vma=False)
```

profile of v0, /device:TPU:0, one launch (start us, length us, event | category | flops | bytes accessed | tf_op | source)
XLA Modules:
  0.0 1611.5 jit_solution(3980976646652202752)
XLA Ops:
  28.3 5.1 reshape.334
  33.4 5.1 copy.415
  50.8 159.2 %all-gather.3.cloned.1.call-done = bf16[3,4608,512]{2,1,0:T(8,128)(2,1)} async-done(((bf16[3,576,512]{2,1,0:T(8,128)(2,1)}), bf16[3,4608,512]{2,1,0:T(8,128)(2,1)}) %all-gather.3.cloned.1.call-update) | async-done | bytes 14155792 | tf_op jit(solution)/shard_map/all_gather | solution.py:90
  210.0 9.5 fusion.277
  232.7 34.9 %all-gather.5.cloned.1.call-done = bf16[917504]{0:T(1024)(128)(2,1)} async-done(((bf16[28672]{0:T(1024)(128)(2,1)}), bf16[917504]{0:T(1024)(128)(2,1)}) %all-gather.5.cloned.1.call-update) | async-done | bytes 1835024 | tf_op jit(solution)/shard_map/all_gather | solution.py:91
  305.2 5.5 fusion.102
  316.1 5.2 copy.320
  326.1 5.2 copy.321
  331.3 5.9 fusion
  337.2 5.2 copy.323
  342.3 8.9 convert_reduce_fusion
  403.2 8.5 fusion.86
  434.0 18.0 %pad_maximum_fusion = f32[3,4608,512]{2,1,0:T(8,128)} fusion(f32[1,4608,512]{2,1,0:T(8,128)} %bitcast.102, f32[1,4608,512]{2,1,0:T(8,128)} %bitcast.83, f32[1,4608,512]{2,1,0:T(8,128)S(1)} %bitcast.424), kind=kLoop, calls=%fused_computation.3 | loop fusion | flops 14155776 | bytes 56623104 | tf_op jit(solution)/shard_map/stack | solution.py:152
  456.3 447.8 %reduce-scatter.2.cloned.1.call-done = f32[3,576,512]{2,1,0:T(8,128)} async-done(((f32[3,4608,512]{2,1,0:T(8,128)}), f32[3,576,512]{2,1,0:T(8,128)}) %reduce-scatter.2.cloned.1.call-update) | async-done | bytes 3538960 | tf_op jit(solution)/shard_map/reduce_scatter | solution.py:153
  926.8 56.1 %all-reduce.15.cloned.1.call-done = (bf16[4,128,1792]{2,1,0:T(8,128)(2,1)}, bf16[3,576,512]{2,1,0:T(8,128)(2,1)}) async-done(((bf16[4,128,1792]{2,1,0:T(8,128)(2,1)}, bf16[3,576,512]{2,1,0:T(8,128)(2,1)}), (bf16[4,128,1792]{2,1,0:T(8,128)(2,1)}, bf16[3,576,512]{2,1,0:T(8,128)(2,1)})) %all-reduce.15.cloned.1.call-update) | async-done | bytes 3604496 | tf_op jit(solution)/shard_map/psum | solution.py:122
  982.9 5.1 convolution_multiply_fusion
  993.3 41.7 %psum.30 = f32[5120]{0:T(1024)} all-reduce(f32[5120]{0:T(1024)} %constant_dynamic-update-slice_fusion.1), channel_id=1, replica_groups=mesh['scale'=4,'space'=8] {'scale','space'}, use_global_device_ids=true, to_apply=%region_12.13 | all-reduce | flops 5120 | bytes 40960 | tf_op jit(solution)/shard_map/psum | solution.py:162
  1042.6 5.3 fusion.73
  1056.4 9.9 multiply_subtract_fusion
  1066.4 85.7 %all-reduce.13.cloned.1.call-done = (f32[917504]{0:T(1024)}, f32[3,512,512]{2,1,0:T(8,128)}) async-done(((f32[917504]{0:T(1024)}, f32[3,512,512]{2,1,0:T(8,128)}), (f32[917504]{0:T(1024)}, f32[3,512,512]{2,1,0:T(8,128)})) %all-reduce.13.cloned.1.call-update) | async-done | bytes 6815760
  1155.7 5.5 fusion.286
  1162.8 7.4 fusion.287
  1179.1 35.2 %custom-call.35 = f32[3,128,128]{2,1,0:T(8,128)S(1)} custom-call(f32[3,128,128]{2,1,0:T(8,128)S(1)} %cholesky.274), custom_call_target="Cholesky" | custom-call | tf_op jit(solution)/shard_map/jit(cholesky)/cholesky | solution.py:63
  1214.3 30.1 %custom-call.36 = f32[3,1,128,128]{2,3,1,0:T(8,128)} custom-call(f32[3,1,128,128]{3,2,1,0:T(8,128)S(1)} %select_bitcast_fusion.2), custom_call_target="InvertDiagBlocksLowerTriangular" | custom-call | tf_op jit(solution)/shard_map/jit(cholesky)/cholesky | solution.py:63
  1252.4 36.4 %custom-call.37 = f32[3,128,128]{2,1,0:T(8,128)S(1)} custom-call(f32[3,128,128]{2,1,0:T(8,128)} %cholesky.278), custom_call_target="Cholesky" | custom-call | tf_op jit(solution)/shard_map/jit(cholesky)/cholesky | solution.py:63
  1289.6 30.9 %custom-call.38 = f32[3,1,128,128]{2,3,1,0:T(8,128)} custom-call(f32[3,1,128,128]{3,2,1,0:T(8,128)} %get-tuple-element.142), custom_call_target="InvertDiagBlocksLowerTriangular" | custom-call | tf_op jit(solution)/shard_map/jit(cholesky)/cholesky | solution.py:63
  1326.5 36.6 %custom-call.39 = f32[3,128,128]{2,1,0:T(8,128)} custom-call(f32[3,128,128]{2,1,0:T(8,128)} %cholesky.283), custom_call_target="Cholesky" | custom-call | tf_op jit(solution)/shard_map/jit(cholesky)/cholesky | solution.py:63
  1364.9 31.1 %custom-call.40 = f32[3,1,128,128]{2,3,1,0:T(8,128)} custom-call(f32[3,1,128,128]{3,2,1,0:T(8,128)} %get-tuple-element.140), custom_call_target="InvertDiagBlocksLowerTriangular" | custom-call | tf_op jit(solution)/shard_map/jit(cholesky)/cholesky | solution.py:63
  1401.0 36.6 %custom-call.41 = f32[3,128,128]{2,1,0:T(8,128)} custom-call(f32[3,128,128]{2,1,0:T(8,128)} %convolution_subtract_fusion.3), custom_call_target="Cholesky" | custom-call | tf_op jit(solution)/shard_map/jit(cholesky)/cholesky | solution.py:63
  1443.9 14.8 while.1
  1458.7 119.5 %custom-call.42 = f32[3,4,128,128]{2,3,1,0:T(8,128)} custom-call(f32[3,4,128,128]{3,2,1,0:T(8,128)} %bitcast.443), custom_call_target="InvertDiagBlocksLowerTriangular" | custom-call | tf_op jit(solution)/shard_map/vmap(jit(_solve_triangular))/triangular_solve | solution.py:65
  1588.6 5.2 fusion.77
  (365 shorter events, 294.0 us)
Async XLA Ops:
  7.2 1042.1 %copy-start = (f32[3,512,512]{2,1,0:T(8,128)S(1)}, f32[3,512,512]{2,1,0:T(8,128)}, u32[]{:S(2)}) copy-start(f32[3,512,512]{2,1,0:T(8,128)} %param.26) | copy-start | bytes 9437188
  7.2 13.6 copy-start.50
  7.2 14.4 copy-start.71
  7.2 15.0 copy-start.55
  7.2 202.8 %all-gather.3.cloned.1.call-start = ((), (), s32[]{:S(2)}) async-start(), calls=%async_computation.1 | async-start | bytes 15925248 | tf_op jit(solution)/shard_map/all_gather | solution.py:90
  10.9 256.8 %all-gather.5.cloned.1.call-start = ((), (), s32[]{:S(2)}) async-start(), calls=%async_computation.2 | async-start | bytes 1892352 | tf_op jit(solution)/shard_map/all_gather | solution.py:91
  14.7 23.9 %collective-permute-start = (bf16[1,128,512]{1,2,0:T(8,128)(2,1)}, bf16[1,128,512]{1,2,0:T(8,128)(2,1)S(1)}, u32[]{:S(2)}, u32[]{:S(2)}) collective-permute-start(bf16[1,128,512]{1,2,0:T(8,128)(2,1)} %get-tuple-element.137), channel_id=1, source_target_pairs={{0,1},{1,2},{2,3},{3,4},{4,5},{5,6},{6,7},{8,9},{9,10},{10,11},{11... | collective-permute-start | bytes 393224 | tf_op jit(solution)/shard_map/ppermute | solution.py:26
  19.5 19.0 %collective-permute-start.1 = (bf16[1,128,512]{1,2,0:T(8,128)(2,1)}, bf16[1,128,512]{1,2,0:T(8,128)(2,1)S(1)}, u32[]{:S(2)}, u32[]{:S(2)}) collective-permute-start(bf16[1,128,512]{1,2,0:T(8,128)(2,1)} %get-tuple-element.138), channel_id=1, source_target_pairs={{1,0},{2,1},{3,2},{4,3},{5,4},{6,5},{7,6},{9,8},{10,9},{11,10},{12... | collective-permute-start | bytes 393224 | tf_op jit(solution)/shard_map/ppermute | solution.py:29
  21.5 882.5 %reduce-scatter.2.cloned.1.call-start = ((), (), s32[]{:S(2)}) async-start(), calls=%async_computation.3 | async-start | bytes 31850496 | tf_op jit(solution)/shard_map/reduce_scatter | solution.py:153
  22.9 10.6 copy-start.56
  24.1 9.3 copy-start.69
  24.1 281.1 %copy-start.62 = (f32[4]{0:T(128)}, f32[4]{0:T(128)S(1)}, u32[]{:S(2)}) copy-start(f32[4]{0:T(128)S(1)} %get-tuple-element.115) | copy-start | bytes 52
  38.5 184.7 %copy-start.58 = (f32[512]{0:T(512)}, f32[512]{0:T(512)S(1)}, u32[]{:S(2)}) copy-start(f32[512]{0:T(512)S(1)} %get-tuple-element.148) | copy-start | bytes 6148
  38.5 249.8 %copy-start.60 = (f32[512]{0:T(512)}, f32[512]{0:T(512)S(1)}, u32[]{:S(2)}) copy-start(f32[512]{0:T(512)S(1)} %get-tuple-element.147) | copy-start | bytes 6148
  38.6 266.7 %copy-start.65 = (f32[512]{0:T(512)}, f32[512]{0:T(512)S(1)}, u32[]{:S(2)}) copy-start(f32[512]{0:T(512)S(1)} %get-tuple-element.146) | copy-start | bytes 6148
  50.8 168.7 %copy-start.73 = (pred[8,17]{0,1:T(8,128)(4,1)S(1)}, pred[8,17]{0,1:T(8,128)(4,1)}, u32[]{:S(2)}) copy-start(pred[8,17]{0,1:T(8,128)(4,1)} %constant.299) | copy-start | bytes 412
  210.0 9.5 copy-start.40
  226.3 50.4 %collective-permute-start.2 = (bf16[1,128,512]{2,1,0:T(8,128)(2,1)}, bf16[1,128,512]{2,1,0:T(8,128)(2,1)}, u32[]{:S(2)}, u32[]{:S(2)}) collective-permute-start(bf16[1,128,512]{2,1,0:T(8,128)(2,1)} %get-tuple-element.135), channel_id=1, source_target_pairs={{0,1},{1,2},{2,3},{3,4},{4,5},{5,6},{6,7},{8,9},{9,10},{10,11},{11... | collective-permute-start | bytes 393224 | tf_op jit(solution)/shard_map/ppermute | solution.py:26
  229.3 47.4 %collective-permute-start.3 = (bf16[1,128,512]{2,1,0:T(8,128)(2,1)}, bf16[1,128,512]{2,1,0:T(8,128)(2,1)S(1)}, u32[]{:S(2)}, u32[]{:S(2)}) collective-permute-start(bf16[1,128,512]{2,1,0:T(8,128)(2,1)} %get-tuple-element.136), channel_id=1, source_target_pairs={{1,0},{2,1},{3,2},{4,3},{5,4},{6,5},{7,6},{9,8},{10,9},{11,10},{12... | collective-permute-start | bytes 393224 | tf_op jit(solution)/shard_map/ppermute | solution.py:29
  288.4 11.5 copy-start.13
  288.9 10.7 copy-start.9
  289.0 6.9 collective-permute-start.4
  292.4 7.3 collective-permute-start.5
  353.8 18.3 %collective-permute-start.6 = (bf16[1,128,512]{2,1,0:T(8,128)(2,1)S(1)}, bf16[1,128,512]{2,1,0:T(8,128)(2,1)S(1)}, u32[]{:S(2)}, u32[]{:S(2)}) collective-permute-start(bf16[1,128,512]{2,1,0:T(8,128)(2,1)S(1)} %get-tuple-element.131), channel_id=1, source_target_pairs={{0,1},{1,2},{2,3},{3,4},{4,5},{5,6},{6,7},{8,9},{9,10},{10,11},{11... | collective-permute-start | bytes 393224 | tf_op jit(solution)/shard_map/ppermute | solution.py:26
  357.1 15.0 collective-permute-start.7
  385.3 12.7 copy-start.29
  385.4 12.6 collective-permute-start.8
  389.9 8.1 collective-permute-start.9
  452.0 530.8 %all-reduce.15.cloned.1.call-start = ((), (), s32[]{:S(2)}) async-start(), calls=%async_computation.5 | async-start | bytes 7208960 | tf_op jit(solution)/shard_map/psum | solution.py:122
  907.5 244.5 %all-reduce.13.cloned.1.call-start = ((), (), s32[]{:S(2)}) async-start(), calls=%async_computation.4 | async-start | bytes 13631488
  920.8 115.6 %collective-permute-start.10 = (bf16[1,128,512]{2,1,0:T(8,128)(2,1)}, bf16[1,128,512]{2,1,0:T(8,128)(2,1)S(1)}, u32[]{:S(2)}, u32[]{:S(2)}) collective-permute-start(bf16[1,128,512]{2,1,0:T(8,128)(2,1)} %get-tuple-element.127), channel_id=1, source_target_pairs={{0,1},{1,2},{2,3},{3,4},{4,5},{5,6},{6,7},{8,9},{9,10},{10,11},{11... | collective-permute-start | bytes 393224 | tf_op jit(solution)/shard_map/ppermute | solution.py:26
  924.2 112.2 %collective-permute-start.11 = (bf16[1,128,512]{2,1,0:T(8,128)(2,1)S(1)}, bf16[1,128,512]{2,1,0:T(8,128)(2,1)S(1)}, u32[]{:S(2)}, u32[]{:S(2)}) collective-permute-start(bf16[1,128,512]{2,1,0:T(8,128)(2,1)S(1)} %get-tuple-element.128), channel_id=1, source_target_pairs={{1,0},{2,1},{3,2},{4,3},{5,4},{6,5},{7,6},{9,8},{10,9},{11,10},{12... | collective-permute-start | bytes 393224 | tf_op jit(solution)/shard_map/ppermute | solution.py:29
  (61 other events, 241.6 us)
Sparse Core Ops, SparseCore 0:
  11.0 198.9 all-gather.2
  213.5 54.0 all-gather.4
  452.1 451.8 reduce-scatter.1
  907.7 75.1 all-reduce.14
  989.1 162.8 all-reduce.12
where the time goes:
time: 1620 us; the launch traced here: 1610 us
  waiting for transfers between devices  787 us (49%)
  other arithmetic  446 us (28%)
  local copies, waits for them, and re-layouts  156 us (10%)
  matrix products  134 us (8%)
  blocking collectives  41.7 us (3%)
  starting transfers between devices  31.3 us (2%)
    reduce_scatter x1, waiting for transfers between devices, local(): lax.psum_scatter(stacked_grads, 'space', scatter_dimension=1, tiled=True)  448 us
    another operation x16, other arithmetic, renew(): lower = jnp.linalg.cholesky(gram)  242 us
    all_gather x1, waiting for transfers between devices, local(): lax.all_gather(conv_master.astype(jnp.bfloat16), 'space', axis=1, tiled=T...  159 us
    another operation x4, other arithmetic, renew(): jax.scipy.linalg.solve_triangular(factor, matrix.T, lower=True)  125 us
    unnamed x6, waiting for transfers between devices  85.7 us
    psum x1, waiting for transfers between devices, local(): merged = lax.psum(term.astype(jnp.bfloat16), 'scale')  56.1 us
    psum x1, blocking collectives, local(): lax.psum((partial_stats, vec_partial), ('scale', 'space'))  41.7 us
    all_gather x1, waiting for transfers between devices, local(): lax.all_gather(head_master.astype(jnp.bfloat16), ('scale', 'space'), axis...  34.9 us
  transfers between devices with their start and end apart: 17, of which 6 were waited for; matrix products, arithmetic and copies ran while one was open for 8% of the time, Pallas kernels for 0%

commit v1 on v0

--- a/solution.py
+++ b/solution.py
@@ -1,4 +1,8 @@
+from functools import partial
+
 import jax
+import jax.experimental.pallas as pl
+import jax.experimental.pallas.tpu as pltpu
 import jax.numpy as jnp
 from jax import lax
 from jax.sharding import PartitionSpec as P
@@ -16,6 +20,478 @@
 RATE_HEAD = 0.08
 RATE_BIAS = 0.5
 RATE_GAIN = 20.0
+VMEM_LIMIT = 60 * 2**20
+
+
+MESH = pl.DeviceIdType.MESH
+LANES = 128
+
+
+def place():
+    scale, space = lax.axis_index("scale"), lax.axis_index("space")
+    across, core = scale // 2, lax.rem(scale, 2)
+    deep, side = space // 2, lax.rem(space, 2)
+    return (across, core, deep, side)
+
+
+def at(across, core, deep, side):
+    return (2 * across + core, 2 * deep + side)
+
+
+def greet(peers):
+    barrier = pltpu.get_barrier_semaphore()
+    for peer in peers:
+        pl.semaphore_signal(barrier, inc=1, device_id=peer, device_id_type=MESH)
+    pl.semaphore_wait(barrier, len(peers))
+
+
+def remote(source, target, send, receive, device):
+    return pltpu.make_async_remote_copy(
+        src_ref=source,
+        dst_ref=target,
+        send_sem=send,
+        recv_sem=receive,
+        device_id=device,
+        device_id_type=MESH,
+    )
+
+
+def lanes(index, count=1):
+    return pl.ds(pl.multiple_of(index * LANES, LANES), count * LANES)
+
+
+def partners(deep_count):
+    across, core, deep, side = place()
+    peers = [
+        at(across, 1 - core, deep, side),
+        at(1 - across, core, deep, side),
+        at(across, core, deep, 1 - side),
+    ]
+    peers += [
+        at(across, core, lax.rem(deep + hop, deep_count), side) for hop in range(1, deep_count)
+    ]
+    return peers
+
+
+def gather_kernel(layers, deep_count, master, full, own, local_sem, sends, receives):
+    across, core, deep, side = place()
+    block = 2 * core + across
+    greet(partners(deep_count))
+
+    def chunk_of(hop):
+        source = lax.rem(deep - hop + deep_count, deep_count)
+        return (source, lax.rem(source, 2))
+
+    def first(layer, hop):
+        piece = own.at[layer, :, lanes(block)]
+        target = full.at[layer, deep, side, :, lanes(block)]
+        to = at(across, core, lax.rem(deep + hop, deep_count), side)
+        return remote(piece, target, sends.at[0, layer, hop], receives.at[0, layer, hop], to)
+
+    def first_in(layer, hop):
+        source, unused = chunk_of(hop)
+        piece = full.at[layer, source, side, :, lanes(block)]
+        return remote(
+            piece, piece, sends.at[0, layer, hop], receives.at[0, layer, hop], at(across, core, deep, side)
+        )
+
+    def second(layer, hop, incoming):
+        source, odd = chunk_of(hop)
+        there_side = lax.rem(side + 1 - odd, 2)
+        there_across = lax.rem(across + odd, 2)
+        to = at(there_across, core, deep, there_side)
+        if incoming:
+            piece = full.at[layer, source, there_side, :, lanes(2 * core + there_across)]
+        else:
+            piece = full.at[layer, source, side, :, lanes(block)]
+        return remote(piece, piece, sends.at[1, layer, hop], receives.at[1, layer, hop], to)
+
+    def third(layer, hop, half, incoming):
+        source, odd = chunk_of(hop)
+        there_side = lax.rem(side + odd, 2)
+        there_across = lax.rem(across + 1 - odd, 2)
+        to = at(there_across, core, deep, there_side)
+        here = there_side if incoming else side
+        lane = there_across if incoming else across
+        piece_side = (1 - odd) * half + odd * here
+        piece_lane = 2 * core + (1 - odd) * lane + odd * half
+        piece = full.at[layer, source, piece_side, :, lanes(piece_lane)]
+        return remote(
+            piece, piece, sends.at[2 + half, layer, hop], receives.at[2 + half, layer, hop], to
+        )
+
+    def fourth(layer, hop, incoming):
+        source, unused = chunk_of(hop)
+        column = 1 - core if incoming else core
+        piece = full.at[layer, source, :, :, lanes(2 * column, 2)]
+        to = at(across, 1 - core, deep, side)
+        return remote(piece, piece, sends.at[4, layer, hop], receives.at[4, layer, hop], to)
+
+    def local(layer):
+        return pltpu.make_async_copy(
+            own.at[layer, :, lanes(block)],
+            full.at[layer, deep, side, :, lanes(block)],
+            local_sem.at[layer],
+        )
+
+    def each(low, action):
+        def step(hop, carry):
+            action(hop)
+            return carry
+
+        lax.fori_loop(low, deep_count, step, 0)
+
+    for layer in range(layers):
+        own[layer] = master[layer].astype(jnp.bfloat16)
+        local(layer).start()
+        each(1, lambda hop: first(layer, hop).start())
+
+    def go_second(layer):
+        local(layer).wait()
+        second(layer, 0, False).start()
+
+        def step(hop):
+            first_in(layer, hop).wait_recv()
+            second(layer, hop, False).start()
+
+        each(1, step)
+
+    def go_third(layer):
+        def step(hop):
+            second(layer, hop, True).wait_recv()
+            third(layer, hop, 0, False).start()
+            third(layer, hop, 1, False).start()
+
+        each(0, step)
+
+    def go_fourth(layer):
+        def step(hop):
+            third(layer, hop, 0, True).wait_recv()
+            third(layer, hop, 1, True).wait_recv()
+            fourth(layer, hop, False).start()
+
+        each(0, step)
+
+    stages = [go_second, go_third, go_fourth]
+    for turn in range(layers + 2):
+        for lag in (0, 1, 2):
+            if 0 <= turn - lag < layers:
+                stages[lag](turn - lag)
+
+    for layer in range(layers):
+
+        def finish(hop):
+            fourth(layer, hop, True).wait_recv()
+            second(layer, hop, False).wait_send()
+            third(layer, hop, 0, False).wait_send()
+            third(layer, hop, 1, False).wait_send()
+            fourth(layer, hop, False).wait_send()
+
+        each(0, finish)
+        each(1, lambda hop: first(layer, hop).wait_send())
+
+
+def gather_weights(master, space_count):
+    layers, rows, columns = master.shape
+    deep_count = space_count // 2
+    full = pl.pallas_call(
+        partial(gather_kernel, layers, deep_count),
+        out_shape=jax.ShapeDtypeStruct((layers, deep_count, 2, rows, columns), jnp.bfloat16),
+        in_specs=[pl.BlockSpec(memory_space=pltpu.VMEM)],
+        out_specs=pl.BlockSpec(memory_space=pl.ANY),
+        scratch_shapes=[
+            pltpu.VMEM((layers, rows, columns), jnp.bfloat16),
+            pltpu.SemaphoreType.DMA((layers,)),
+            pltpu.SemaphoreType.DMA((5, layers, deep_count)),
+            pltpu.SemaphoreType.DMA((5, layers, deep_count)),
+        ],
+        compiler_params=pltpu.CompilerParams(
+            collective_id=0, has_side_effects=True, vmem_limit_bytes=VMEM_LIMIT
+        ),
+    )(master)
+    return full.reshape(layers, space_count * rows, columns)
+
+
+def reduce_kernel(
+    layers, deep_count, grads, total, mine, core_in, second_in, kept, third_in, last, last_in, acc, local_sem, sends, receives
+):
+    across, core, deep, side = place()
+    block = 2 * core + across
+    steps = layers * deep_count
+
+    def split(step):
+        layer, hop = step // deep_count, lax.rem(step, deep_count)
+        target = lax.rem(deep + hop, deep_count)
+        return (layer, hop, target, lax.rem(target, 2))
+
+    def first(step):
+        layer, hop, target, odd = split(step)
+        return remote(
+            grads.at[layer, target, :, :, lanes(2 * (1 - core), 2)],
+            core_in.at[step],
+            sends.at[0, step],
+            receives.at[0, step],
+            at(across, 1 - core, deep, side),
+        )
+
+    def load(step):
+        layer, hop, target, odd = split(step)
+        return pltpu.make_async_copy(
+            grads.at[layer, target, :, :, lanes(2 * core, 2)], mine.at[step], local_sem.at[step]
+        )
+
+    def second(step, half):
+        layer, hop, target, odd = split(step)
+        piece_side = (1 - odd) * half + odd * (1 - side)
+        piece_lane = (1 - odd) * (1 - across) + odd * half
+        to = at(lax.rem(across + 1 - odd, 2), core, deep, lax.rem(side + odd, 2))
+        return remote(
+            mine.at[step, piece_side, :, lanes(piece_lane)],
+            second_in.at[step, half],
+            sends.at[1 + half, step],
+            receives.at[1 + half, step],
+            to,
+        )
+
+    def third(step):
+        layer, hop, target, odd = split(step)
+        keep = (1 - odd) * side + odd * across
+        to = at(lax.rem(across + odd, 2), core, deep, lax.rem(side + 1 - odd, 2))
+        return remote(
+            kept.at[step, 1 - keep],
+            third_in.at[step],
+            sends.at[3, step],
+            receives.at[3, step],
+            to,
+        )
+
+    def fourth(step):
+        layer, hop, target, odd = split(step)
+        return remote(
+            last.at[step],
+            last_in.at[step],
+            sends.at[4, step],
+            receives.at[4, step],
+            at(across, core, target, side),
+        )
+
+    def fifth(layer, incoming):
+        lane = 2 * core + (1 - across if incoming else across)
+        piece = total.at[layer, :, lanes(lane)]
+        to = at(1 - across, core, deep, side)
+        return remote(piece, piece, sends.at[5, layer], receives.at[5, layer], to)
+
+    def sixth(layer, incoming):
+        column = 1 - core if incoming else core
+        piece = total.at[layer, :, lanes(2 * column, 2)]
+        to = at(across, 1 - core, deep, side)
+        return remote(piece, piece, sends.at[6, layer], receives.at[6, layer], to)
+
+    def run(low, high, action):
+        def body(step, carry):
+            action(step)
+            return carry
+
+        lax.fori_loop(low, high, body, 0)
+
+    run(0, steps, lambda step: load(step).start())
+    greet(partners(deep_count))
+    run(0, steps, lambda step: first(step).start())
+
+    def wide(left, right):
+        return left.astype(jnp.float32) + right.astype(jnp.float32)
+
+    def go_second(step):
+        load(step).wait()
+        first(step).wait_recv()
+        mine[step] = wide(mine[step], core_in[step]).astype(jnp.bfloat16)
+        second(step, 0).start()
+        second(step, 1).start()
+
+    def go_third(step):
+        layer, hop, target, odd = split(step)
+        for half in range(2):
+            second(step, half).wait_recv()
+            keep_side = (1 - odd) * half + odd * side
+            keep_lane = (1 - odd) * across + odd * half
+            kept[step, half] = wide(
+                mine[step, keep_side, :, lanes(keep_lane)], second_in[step, half]
+            ).astype(jnp.bfloat16)
+        third(step).start()
+
+    def go_fourth(step):
+        layer, hop, target, odd = split(step)
+        third(step).wait_recv()
+        keep = (1 - odd) * side + odd * across
+        last[step] = wide(kept[step, keep], third_in[step]).astype(jnp.bfloat16)
+
+        @pl.when(hop > 0)
+        def unused():
+            fourth(step).start()
+
+    lag_third, lag_fourth = 2, 4
+
+    def turn(step):
+        @pl.when(step < steps)
+        def go():
+            go_second(step)
+
+        @pl.when(jnp.logical_and(step >= lag_third, step < steps + lag_third))
+        def go_next():
+            go_third(step - lag_third)
+
+        @pl.when(step >= lag_fourth)
+        def go_last():
+            go_fourth(step - lag_fourth)
+
+    run(0, steps + lag_fourth, turn)
+
+    def close(layer):
+        acc[...] = last[layer * deep_count].astype(jnp.float32)
+
+        def add(hop):
+            step = layer * deep_count + hop
+            fourth(step).wait_recv()
+            acc[...] += last_in[step].astype(jnp.float32)
+
+        run(1, deep_count, add)
+        total[layer, :, lanes(block)] = acc[...].astype(jnp.bfloat16)
+        fifth(layer, False).start()
+
+    def spread(layer):
+        fifth(layer, True).wait_recv()
+        sixth(layer, False).start()
+
+    run(0, layers, close)
+    run(0, layers, spread)
+
+    def finish(layer):
+        sixth(layer, True).wait_recv()
+        fifth(layer, False).wait_send()
+        sixth(layer, False).wait_send()
+
+    run(0, layers, finish)
+
+    def drain(step):
+        layer, hop, target, odd = split(step)
+        first(step).wait_send()
+        second(step, 0).wait_send()
+        second(step, 1).wait_send()
+        third(step).wait_send()
+
+        @pl.when(hop > 0)
+        def unused():
+            fourth(step).wait_send()
+
+    run(0, steps, drain)
+
+
+def reduce_grads(grads, space_count):
+    layers, all_rows, columns = grads.shape
+    deep_count, rows = space_count // 2, all_rows // space_count
+    steps = layers * deep_count
+    low = jnp.bfloat16
+    return pl.pallas_call(
+        partial(reduce_kernel, layers, deep_count),
+        out_shape=jax.ShapeDtypeStruct((layers, rows, columns), low),
+        in_specs=[pl.BlockSpec(memory_space=pl.ANY)],
+        out_specs=pl.BlockSpec(memory_space=pltpu.VMEM),
+        scratch_shapes=[
+            pltpu.VMEM((steps, 2, rows, 2 * LANES), low),
+            pltpu.VMEM((steps, 2, rows, 2 * LANES), low),
+            pltpu.VMEM((steps, 2, rows, LANES), low),
+            pltpu.VMEM((steps, 2, rows, LANES), low),
+            pltpu.VMEM((steps, rows, LANES), low),
+            pltpu.VMEM((steps, rows, LANES), low),
+            pltpu.VMEM((steps, rows, LANES), low),
+            pltpu.VMEM((rows, LANES), jnp.float32),
+            pltpu.SemaphoreType.DMA((steps,)),
+            pltpu.SemaphoreType.DMA((7, steps)),
+            pltpu.SemaphoreType.DMA((7, steps)),
+        ],
+        compiler_params=pltpu.CompilerParams(
+            collective_id=1, has_side_effects=True, vmem_limit_bytes=VMEM_LIMIT
+        ),
+    )(grads.reshape(layers, deep_count, 2, rows, columns))
+
+
+HI=lax.Precision.HIGHEST
+def dot(a,b,ca,cb,precision=HI):
+    return lax.dot_general(a,b,(((ca,),(cb,)),((),())),precision=precision,preferred_element_type=jnp.float32)
+
+def eliminate(blocks, off, size):
+    nl=len(blocks); nb=size//8
+    sub=lax.broadcasted_iota(jnp.int32,(8,1),0)
+    for k in range(size):
+        b0=k//8; kr=k%8
+        for l in range(nl):
+            bl=blocks[l]
+            row=bl[b0][kr:kr+1,:]
+            inv=1.0/bl[b0][kr:kr+1,off+k:off+k+1]
+            srow=row*inv
+            for b in range(b0,nb):
+                if b==b0:
+                    if kr==7: continue
+                    col=jnp.where(sub>kr,bl[b][:,off+k:off+k+1],0.0)
+                else:
+                    col=bl[b][:,off+k:off+k+1]
+                bl[b]=bl[b]-col*srow
+    out=[]
+    lane=lax.broadcasted_iota(jnp.int32,(8,blocks[0][0].shape[1]),1)
+    row8=lax.broadcasted_iota(jnp.int32,(8,blocks[0][0].shape[1]),0)
+    for l in range(nl):
+        res=[]
+        for b in range(nb):
+            v=blocks[l][b]
+            d=jnp.sum(jnp.where(lane==row8+(off+8*b),v,0.0),1,keepdims=True)
+            res.append(v*lax.rsqrt(d))
+        out.append(jnp.concatenate(res,0))
+    return out
+
+def renew_kernel(layers, B, sum_ref, stat_ref, base_ref, sn_ref, bn_ref, m_ref, row_ref):
+    C=stat_ref.shape[-1]
+    D=128
+    for l in range(layers):
+        sn=BETA_TWO*stat_ref[l]+(1.0-BETA_TWO)*sum_ref[l]
+        sn_ref[l]=sn
+        pt=dot(base_ref[l],sn,0,0)
+        m_ref[l,:,C:2*C]=pt
+        m_ref[l,:,0:C]=dot(pt,pt,1,1)
+    eye=(lax.broadcasted_iota(jnp.int32,(D,D),0)==lax.broadcasted_iota(jnp.int32,(D,D),1)).astype(jnp.float32)
+    def outer(k,c):
+        ks=pl.ds(pl.multiple_of(k*D,D),D)
+        panels=[jnp.concatenate([m_ref[l,ks,ks],eye],1) for l in range(layers)]
+        invs=[]
+        done=[[] for _ in range(layers)]
+        for j in range(D//B):
+            blocks=[[p[8*i:8*i+8] for i in range(B//8)] for p in panels]
+            tops=eliminate(blocks,B*j,B)
+            for l in range(layers):
+                done[l].append(tops[l][:,D:])
+                if j<D//B-1:
+                    panels[l]=panels[l][B:]-dot(tops[l][:,B*(j+1):D],tops[l],0,0)
+        for l in range(layers):
+            linv=jnp.concatenate(done[l],0)
+            row_ref[l]=dot(linv,m_ref[l,ks,:],1,0)
+            m_ref[l,ks,C:2*C]=row_ref[l,:,C:2*C]
+        def inner(i,c2):
+            is_=pl.ds(pl.multiple_of(i*D,D),D)
+            for l in range(layers):
+                m_ref[l,is_,:]=m_ref[l,is_,:]-dot(row_ref[l,:,is_],row_ref[l],0,0)
+            return c2
+        lax.fori_loop(k+1,C//D,inner,0)
+        return c
+    lax.fori_loop(0,C//D,outer,0)
+    for l in range(layers):
+        bn_ref[l]=m_ref[l,:,C:2*C].T
+
+def renew(summed, statistics, bases, B=64):
+    L,C,_=statistics.shape
+    v=pl.BlockSpec(memory_space=pltpu.VMEM)
+    sh=jax.ShapeDtypeStruct((L,C,C),jnp.float32)
+    return pl.pallas_call(partial(renew_kernel,L,B),out_shape=(sh,sh),in_specs=[v]*3,out_specs=[v]*2,
+      scratch_shapes=[pltpu.VMEM((L,C,2*C),jnp.float32),pltpu.VMEM((L,128,2*C),jnp.float32)],
+      compiler_params=pltpu.CompilerParams(vmem_limit_bytes=VMEM_LIMIT))(summed,statistics,bases)
 
 
 def padded_2(block, sides, width):
@@ -55,16 +531,6 @@
         / (jnp.sqrt(second_new / (1.0 - BETA_TWO**STEP)) + EPSILON)
     )
     return (first_new, second_new, direction)
-
-
-def renew(stats_new, bases):
-    product = jnp.einsum("lcd,lde->lce", stats_new, bases, precision=lax.Precision.HIGHEST)
-    gram = jnp.einsum("lce,lcf->lef", product, product, precision=lax.Precision.HIGHEST)
-    lower = jnp.linalg.cholesky(gram)
-    solved = jax.vmap(
-        lambda factor, matrix: jax.scipy.linalg.solve_triangular(factor, matrix.T, lower=True)
-    )(lower, product)
-    return jnp.transpose(solved, (0, 2, 1))
 
 
 def local(
@@ -87,7 +553,7 @@
     rows_dev = features.shape[1]
     width = features.shape[2]
     head_width = cotangent.shape[2]
-    conv_used = lax.all_gather(conv_master.astype(jnp.bfloat16), "space", axis=1, tiled=True)
+    conv_used = gather_weights(conv_master, lax.axis_size("space"))
     head_flat = lax.all_gather(
         head_master.astype(jnp.bfloat16), ("scale", "space"), axis=0, tiled=True
     )
@@ -149,9 +615,8 @@
         flipped = jnp.transpose(jnp.flip(kernels[which_layer], (0, 1)), (0, 1, 3, 2))
         d_active = convolve_valid(d_padded, flipped)
     features_grad = d_active.astype(jnp.bfloat16)[None]
-    stacked_grads = jnp.stack(conv_grads)
-    conv_part = lax.psum_scatter(stacked_grads, "space", scatter_dimension=1, tiled=True)
-    owned_conv = lax.psum(conv_part.astype(jnp.bfloat16), "scale").astype(jnp.float32)
+    stacked_grads = jnp.stack(conv_grads).astype(jnp.bfloat16)
+    owned_conv = reduce_grads(stacked_grads, lax.axis_size("space")).astype(jnp.float32)
     owned_head = lax.psum_scatter(
         grad_head.reshape(-1), ("scale", "space"), scatter_dimension=0, tiled=True
     )
@@ -174,8 +639,7 @@
         ]
     )
     vec_new = vectors - rates * (vec_dir + DECAY * vectors)
-    stats_new = BETA_TWO * statistics + (1.0 - BETA_TWO) * summed_stats
-    bases_new = renew(stats_new, bases)
+    stats_new, bases_new = renew(summed_stats, statistics, bases)
     return (
         merged,
         features_grad,

time: 1620 us -> 720 us (0.44)
  waiting for transfers between devices: 787 us -> 102 us
  other arithmetic: 446 us -> 45.9 us
  Pallas kernels: 0 us -> 261 us
  local copies, waits for them, and re-layouts: 156 us -> 67.1 us
    reduce_scatter x1 -> x0, waiting for transfers between devices: 448 us -> none  [local(): lax.psum_scatter(stacked_grads, 'space', scatter_dimension=1, tiled=True)]
    another operation x21 -> x1, other arithmetic: 385 us -> 6.86 us  [local(): stacked_grads = jnp.stack(conv_grads).astype(jnp.bfloat16)]
    pallas_call x0 -> x3, Pallas kernels: none -> 261 us  [the longest x1 95.9 us: gather_weights(): pl.pallas_call(partial(gather_kernel, layers, deep_count), out_shape=jax....]
    all_gather x1 -> x0, waiting for transfers between devices: 159 us -> none  [local(): lax.all_gather(conv_master.astype(jnp.bfloat16), 'space', axis=1, tiled=T...]
    conv_general_dilated x6, matrix products: 31.7 us -> 92 us  [convolve_valid(): lax.conv_general_dilated(padded[None], kernel, (1, 1), 'VALID', dimension...]
    psum x1, waiting for transfers between devices: 56.1 us -> 0.01 us  [local(): merged = lax.psum(term.astype(jnp.bfloat16), 'scale')]
    all_gather x1, waiting for transfers between devices: 34.9 us -> 0.02 us  [local(): lax.all_gather(head_master.astype(jnp.bfloat16), ('scale', 'space'), axis...]
    another operation x13 -> x0, matrix products: 30.2 us -> none  [the longest x7 16.4 us: renew(): jax.scipy.linalg.solve_triangular(factor, matrix.T, lower=True)]
  transfers between devices with their start and end apart: 17 -> 15, of which waited for: 6 -> 4; matrix products, arithmetic and copies ran while one was open for 8% -> 21% of each run, Pallas kernels for 0% -> 25%
where the time goes in v1:
time: 720 us; the launch traced here: 715 us
  Pallas kernels  261 us (36%)
  matrix products  148 us (21%)
  waiting for transfers between devices  102 us (14%)
  local copies, waits for them, and re-layouts  67.1 us (9%)
  other arithmetic  45.9 us (6%)
  blocking collectives  43.8 us (6%)
  starting transfers between devices  32 us (4%)
  between operations  15.1 us (2%)
    pallas_call x1, Pallas kernels, gather_weights(): pl.pallas_call(partial(gather_kernel, layers, deep_count), out_shape=jax....  95.9 us
    conv_general_dilated x6, matrix products, convolve_valid(): lax.conv_general_dilated(padded[None], kernel, (1, 1), 'VALID', dimension...  92 us
    unnamed x4, waiting for transfers between devices  90.3 us
    pallas_call x1, Pallas kernels, reduce_grads(): pl.pallas_call(partial(reduce_kernel, layers, deep_count), out_shape=jax....  84.7 us
    pallas_call x1, Pallas kernels, renew(): pl.pallas_call(partial(renew_kernel, L, B), out_shape=(sh, sh), in_specs=...  80.5 us
    psum x1, blocking collectives, local(): lax.psum((partial_stats, vec_partial), ('scale', 'space'))  43.8 us
    ppermute x6, starting transfers between devices, padded_2(): lax.ppermute(lax.slice_in_dim(block, block.shape[dim] - width, None, axis...  23.9 us
    dot_general x27, matrix products, local(): jnp.einsum('rwi,rwo->io', window, d_hidden, preferred_element_type=jnp.fl...  21.4 us
  transfers between devices with their start and end apart: 15, of which 4 were waited for; matrix products, arithmetic and copies ran while one was open for 21% of the time, Pallas kernels for 25%

profile of v1, /device:TPU:0, one launch (start us, length us, event | category | flops | bytes accessed | tf_op | source)
XLA Modules:
  0.0 714.9 jit_solution(4548388363340014657)
XLA Ops:
  8.6 4.9 collective-permute-start
  20.5 95.9 %shard_map.237 = bf16[3,4,2,576,512]{4,3,2,1,0:T(8,128)(2,1)} custom-call(f32[3,576,512]{2,1,0:T(8,128)} %master.1), custom_call_target="tpu_custom_call" | custom-call | tf_op jit(solution)/shard_map/pallas_call | solution.py:197
  116.4 11.4 %fusion.291 = (bf16[1,4,2,576,512]{4,3,2,1,0:T(8,128)(2,1)}, bf16[1,4,2,576,512]{4,3,2,1,0:T(8,128)(2,1)}, bf16[1,4,2,576,512]{4,3,2,1,0:T(8,128)(2,1)}) fusion(bf16[3,4,2,576,512]{4,3,2,1,0:T(8,128)(2,1)} %shard_map.237), kind=kLoop, calls=%fused_computation.379 | loop fusion | bytes 28311552 | tf_op jit(solution)/shard_map/slice | solution.py:574
  130.8 5.1 reshape.185
  135.9 5.1 copy.229
  146.1 18.7 %fusion.299 = f32[1,4,128,512]{3,0,2,1:T(1,128)S(1)} fusion(bf16[1,6,130,512]{3,0,2,1:T(2,128)(2,1)} %copy.172, bf16[3,3,512,512]{3,2,1,0:T(8,128)(2,1)} %bitcast.490), kind=kOutput, calls=%fused_computation.387 | convolution fusion | flops 2415919104 | bytes 6565888 | tf_op jit(solution)/shard_map/conv_general_dilated | solution.py:515
  170.2 7.2 %collective-permute-done.3 = bf16[1,128,512]{2,1,0:T(8,128)(2,1)S(1)} collective-permute-done((bf16[1,128,512]{2,1,0:T(8,128)(2,1)S(1)}, bf16[1,128,512]{2,1,0:T(8,128)(2,1)S(1)}, u32[]{:S(2)}, u32[]{:S(2)}) %collective-permute-start.3) | collective-permute-done | bytes 131104 | tf_op jit(solution)/shard_map/ppermute | solution.py:505
  177.6 17.0 %fusion.32 = f32[1,4,128,512]{3,0,2,1:T(1,128)S(1)} fusion(bf16[3,3,512,512]{3,2,1,0:T(8,128)(2,1)S(1)} %bitcast.494, bf16[1,6,130,512]{3,2,1,0:T(8,128)(2,1)S(1)} %fusion.346), kind=kOutput, calls=%fused_computation.51 | convolution fusion | flops 2415919104 | bytes 6565888 | tf_op jit(solution)/shard_map/conv_general_dilated | solution.py:515
  195.1 4.5 collective-permute-start.4
  202.2 4.4 collective-permute-done.5
  206.8 17.2 %fusion.30 = f32[1,4,128,512]{3,0,2,1:T(1,128)S(1)} fusion(bf16[3,3,512,512]{3,2,1,0:T(8,128)(2,1)S(1)} %bitcast.501, bf16[1,6,130,512]{3,2,1,0:T(8,128)(2,1)S(1)} %fusion.345), kind=kOutput, calls=%fused_computation.49 | convolution fusion | flops 2415919104 | bytes 6565888 | tf_op jit(solution)/shard_map/conv_general_dilated | solution.py:515
  235.2 5.5 copy.176
  243.9 4.8 fusion
  248.7 5.2 copy.179
  256.2 5.1 copy.177
  261.3 9.5 %convert_reduce_fusion = (f32[1792]{0:T(1024)}, bf16[512,1792]{1,0:T(8,128)(2,1)}, f32[1792]{0:T(1024)S(1)}, f32[512,1792]{1,0:T(8,128)}) fusion(f32[512,1792]{1,0:T(8,128)} %copy.177, f32[512,1792]{1,0:T(8,128)} %copy.179, f32[512,1792]{1,0:T(8,128)} %convolution_add_fusion, f32[1792]{0:T(1024)S(1)} %get-tuple-element.105, ...), kind=kLoop, calls=%fused_computation.11 | loop fusion | flops 10088960 | bytes 20206592 | tf_op jit(solution)/shard_map/reduce_sum | solution.py:594
  273.8 4.8 convert_reduce_fusion.1
  279.3 4.0 collective-permute-start.6
  299.0 4.8 reshape.143
  304.1 19.5 %fusion.28 = f32[1,4,128,512]{3,0,2,1:T(1,128)S(1)} fusion(bf16[3,3,512,512]{3,2,1,0:T(8,128)(2,1)} %bitcast.498, bf16[1,6,130,512]{3,2,1,0:T(8,128)(2,1)S(1)} %fusion.197), kind=kOutput, calls=%fused_computation.47 | convolution fusion | flops 2415919104 | bytes 6565888 | tf_op jit(solution)/shard_map/conv_general_dilated | solution.py:515
  324.4 4.6 collective-permute-start.8
  336.2 14.3 %fusion.26 = f32[1,4,128,512]{3,0,2,1:T(1,128)S(1)} fusion(bf16[3,3,512,512]{3,2,1,0:T(8,128)(2,1)S(1)} %bitcast.497, bf16[1,6,130,512]{3,2,1,0:T(8,128)(2,1)S(1)} %fusion.194), kind=kOutput, calls=%fused_computation.45 | convolution fusion | flops 2415919104 | bytes 6565888 | tf_op jit(solution)/shard_map/conv_general_dilated | solution.py:515
  356.3 6.9 pad_maximum_fusion.grads
  363.1 84.7 %shard_map.238 = bf16[3,576,512]{2,1,0:T(8,128)(2,1)} custom-call(bf16[3,4,2,576,512]{4,3,2,1,0:T(8,128)(2,1)} %pad_maximum_fusion.grads), custom_call_target="tpu_custom_call" | custom-call | tf_op jit(solution)/shard_map/pallas_call | solution.py:394
  447.9 5.1 convolution_multiply_fusion
  457.5 43.8 %psum.22 = f32[5120]{0:T(1024)S(1)} all-reduce(f32[5120]{0:T(1024)S(1)} %constant_dynamic-update-slice_fusion.1), channel_id=1, replica_groups=mesh['scale'=4,'space'=8] {'scale','space'}, use_global_device_ids=true, to_apply=%region_10.11 | all-reduce | flops 5120 | bytes 40960 | tf_op jit(solution)/shard_map/psum | solution.py:627
  501.3 4.2 collective-permute-start.10
  507.1 7.9 %fusion.6 = (f32[3,576,512]{2,1,0:T(8,128)S(1)}, f32[3,576,512]{2,1,0:T(8,128)S(1)}) fusion(f32[3,576,512]{2,1,0:T(8,128)} %param.20, f32[3,576,512]{2,1,0:T(8,128)} %param.19, bf16[3,576,512]{2,1,0:T(8,128)(2,1)S(1)} %copy-done.1, f32[3,512,512]{2,1,0:T(8,128)} %base_ref.1), kind=kOutput, calls=%fused_computation.17 | convolution fusion | flops 5442011136 | bytes 19070976 | tf_op jit(solution)/shard_map/lrc,lcd->lrd/dot_general | solution.py:628
  515.1 9.6 %multiply_subtract_fusion = f32[3,576,512]{2,1,0:T(8,128)} fusion(f32[3,576,512]{2,1,0:T(8,128)S(1)} %copy-done.14, f32[3,512,512]{2,1,0:T(8,128)S(1)} %copy-done.2, f32[3,576,512]{2,1,0:T(8,128)S(1)} %get-tuple-element.114, f32[3,576,512]{2,1,0:T(8,128)S(1)} %get-tuple-element.113), kind=kOutput, calls=%fused_computation.18 | convolution fusion | flops 5442895872 | bytes 17301504 | tf_op jit(solution)/shard_map/lrd,lcd->lrc/dot_general | solution.py:630
  526.2 5.2 fusion.38
  532.9 90.2 %all-reduce.13.cloned.1.call-done = (f32[917504]{0:T(1024)}, f32[3,512,512]{2,1,0:T(8,128)}) async-done(((f32[917504]{0:T(1024)}, f32[3,512,512]{2,1,0:T(8,128)}), (f32[917504]{0:T(1024)}, f32[3,512,512]{2,1,0:T(8,128)})) %all-reduce.13.cloned.1.call-update) | async-done | bytes 6815760
  623.1 80.5 %shard_map.239 = (f32[3,512,512]{2,1,0:T(8,128)}, f32[3,512,512]{2,1,0:T(8,128)}) custom-call(f32[3,512,512]{2,1,0:T(8,128)} %get-tuple-element.70.sum_ref, f32[3,512,512]{2,1,0:T(8,128)} %stat_ref.1, f32[3,512,512]{2,1,0:T(8,128)} %base_ref.1), custom_call_target="tpu_custom_call" | custom-call | tf_op jit(solution)/shard_map/pallas_call | solution.py:492
  (227 shorter events, 88.1 us)
Async XLA Ops:
  7.2 220.4 %all-gather.2.cloned.1.call-start = ((), (), s32[]{:S(2)}) async-start(), calls=%async_computation | async-start | bytes 1892352 | tf_op jit(solution)/shard_map/all_gather | solution.py:557
  8.5 159.7 %copy-start.5 = (bf16[1,4,128,512]{2,3,1,0:T(8,128)(2,1)}, bf16[1,4,128,512]{2,3,1,0:T(8,128)(2,1)S(1)}, u32[]{:S(2)}) copy-start(bf16[1,4,128,512]{2,3,1,0:T(8,128)(2,1)S(1)} %copy.168) | copy-start | bytes 1572868
  8.6 133.1 %collective-permute-start = (bf16[1,128,512]{1,2,0:T(8,128)(2,1)S(1)}, bf16[1,128,512]{1,2,0:T(8,128)(2,1)S(1)}, u32[]{:S(2)}, u32[]{:S(2)}) collective-permute-start(bf16[1,128,512]{1,2,0:T(8,128)(2,1)S(1)} %get-tuple-element.102), channel_id=1, source_target_pairs={{0,1},{1,2},{2,3},{3,4},{4,5},{5,6},{6,7},{8,9},{9,10},{10,11},{11... | collective-permute-start | bytes 393224 | tf_op jit(solution)/shard_map/ppermute | solution.py:502
  13.5 128.2 %collective-permute-start.1 = (bf16[1,128,512]{1,2,0:T(8,128)(2,1)S(1)}, bf16[1,128,512]{1,2,0:T(8,128)(2,1)S(1)}, u32[]{:S(2)}, u32[]{:S(2)}) collective-permute-start(bf16[1,128,512]{1,2,0:T(8,128)(2,1)S(1)} %get-tuple-element.103), channel_id=1, source_target_pairs={{1,0},{2,1},{3,2},{4,3},{5,4},{6,5},{7,6},{9,8},{10,9},{11,10},{12... | collective-permute-start | bytes 393224 | tf_op jit(solution)/shard_map/ppermute | solution.py:505
  16.3 606.8 %all-reduce.13.cloned.1.call-start = ((), (), s32[]{:S(2)}) async-start(), calls=%async_computation.2 | async-start | bytes 13631488
  17.1 147.6 %copy-start.42 = (f32[512]{0:T(512)}, f32[512]{0:T(512)S(1)}, u32[]{:S(2)}) copy-start(f32[512]{0:T(512)S(1)} %get-tuple-element.108) | copy-start | bytes 6148
  17.1 177.5 %copy-start.44 = (f32[512]{0:T(512)}, f32[512]{0:T(512)S(1)}, u32[]{:S(2)}) copy-start(f32[512]{0:T(512)S(1)} %get-tuple-element.107) | copy-start | bytes 6148
  17.1 208.1 %copy-start.40 = (f32[512]{0:T(512)}, f32[512]{0:T(512)S(1)}, u32[]{:S(2)}) copy-start(f32[512]{0:T(512)S(1)} %get-tuple-element.106) | copy-start | bytes 6148
  128.5 96.7 %copy-start.35 = (f32[4]{0:T(128)}, f32[4]{0:T(128)S(1)}, u32[]{:S(2)}) copy-start(f32[4]{0:T(128)S(1)} %get-tuple-element.84) | copy-start | bytes 52
  141.6 26.6 %copy-start.19 = (bf16[1,128,512]{1,2,0:T(8,128)(2,1)}, bf16[1,128,512]{1,2,0:T(8,128)(2,1)S(1)}, u32[]{:S(2)}) copy-start(bf16[1,128,512]{1,2,0:T(8,128)(2,1)S(1)} %collective-permute-done.1) | copy-start | bytes 393220
  146.0 31.6 %slice-start = ((s8[4718592]{0:T(1024)(128)(4,1)}), s8[4194304]{0:T(1024)(128)(4,1)S(1)}, s32[]{:S(2)}) async-start(s8[4718592]{0:T(1024)(128)(4,1)} %bitcast.492), calls=%async_computation.3 | async-start | bytes 8388608
  146.0 31.6 %slice-start.1 = ((s8[4718592]{0:T(1024)(128)(4,1)}), s8[524288]{0:T(1024)(128)(4,1)S(1)}, s32[]{:S(2)}) async-start(s8[4718592]{0:T(1024)(128)(4,1)} %bitcast.492), calls=%async_computation.4 | async-start | bytes 1048576
  164.8 29.9 %copy-start.7 = (f32[1,4,128,512]{3,0,2,1:T(1,128)}, f32[1,4,128,512]{3,0,2,1:T(1,128)S(1)}, u32[]{:S(2)}) copy-start(f32[1,4,128,512]{3,0,2,1:T(1,128)S(1)} %fusion.299) | copy-start | bytes 3145732
  165.2 5.0 collective-permute-start.2
  166.9 10.4 %collective-permute-start.3 = (bf16[1,128,512]{2,1,0:T(8,128)(2,1)S(1)}, bf16[1,128,512]{2,1,0:T(8,128)(2,1)S(1)}, u32[]{:S(2)}, u32[]{:S(2)}) collective-permute-start(bf16[1,128,512]{2,1,0:T(8,128)(2,1)S(1)} %get-tuple-element.101), channel_id=1, source_target_pairs={{1,0},{2,1},{3,2},{4,3},{5,4},{6,5},{7,6},{9,8},{10,9},{11,10},{12... | collective-permute-start | bytes 393224 | tf_op jit(solution)/shard_map/ppermute | solution.py:505
  170.2 30.8 %copy-start.23 = (bf16[1,128,512]{2,1,0:T(8,128)(2,1)}, bf16[1,128,512]{2,1,0:T(8,128)(2,1)S(1)}, u32[]{:S(2)}) copy-start(bf16[1,128,512]{2,1,0:T(8,128)(2,1)S(1)} %collective-permute-done.2) | copy-start | bytes 393220
  177.6 29.2 %slice-start.4 = ((s8[4718592]{0:T(1024)(128)(4,1)}), s8[4194304]{0:T(1024)(128)(4,1)S(1)}, s32[]{:S(2)}) async-start(s8[4718592]{0:T(1024)(128)(4,1)} %bitcast.499), calls=%async_computation.7 | async-start | bytes 8388608
  177.6 29.1 %slice-start.5 = ((s8[4718592]{0:T(1024)(128)(4,1)}), s8[524288]{0:T(1024)(128)(4,1)S(1)}, s32[]{:S(2)}) async-start(s8[4718592]{0:T(1024)(128)(4,1)} %bitcast.499), calls=%async_computation.8 | async-start | bytes 1048576
  194.6 29.3 %copy-start.9 = (f32[1,4,128,512]{3,0,2,1:T(1,128)}, f32[1,4,128,512]{3,0,2,1:T(1,128)S(1)}, u32[]{:S(2)}) copy-start(f32[1,4,128,512]{3,0,2,1:T(1,128)S(1)} %fusion.32) | copy-start | bytes 3145732
  195.1 7.0 collective-permute-start.4
  199.7 6.9 collective-permute-start.5
  279.3 24.5 %collective-permute-start.6 = (bf16[1,128,512]{2,1,0:T(8,128)(2,1)}, bf16[1,128,512]{2,1,0:T(8,128)(2,1)S(1)}, u32[]{:S(2)}, u32[]{:S(2)}) collective-permute-start(bf16[1,128,512]{2,1,0:T(8,128)(2,1)} %get-tuple-element.96), channel_id=1, source_target_pairs={{0,1},{1,2},{2,3},{3,4},{4,5},{5,6},{6,7},{8,9},{9,10},{10,11},{11... | collective-permute-start | bytes 393224 | tf_op jit(solution)/shard_map/ppermute | solution.py:502
  283.3 20.5 %collective-permute-start.7 = (bf16[1,128,512]{2,1,0:T(8,128)(2,1)}, bf16[1,128,512]{2,1,0:T(8,128)(2,1)S(1)}, u32[]{:S(2)}, u32[]{:S(2)}) collective-permute-start(bf16[1,128,512]{2,1,0:T(8,128)(2,1)} %get-tuple-element.97), channel_id=1, source_target_pairs={{1,0},{2,1},{3,2},{4,3},{5,4},{6,5},{7,6},{9,8},{10,9},{11,10},{12... | collective-permute-start | bytes 393224 | tf_op jit(solution)/shard_map/ppermute | solution.py:505
  324.4 11.2 %collective-permute-start.8 = (bf16[1,128,512]{2,1,0:T(8,128)(2,1)S(1)}, bf16[1,128,512]{2,1,0:T(8,128)(2,1)S(1)}, u32[]{:S(2)}, u32[]{:S(2)}) collective-permute-start(bf16[1,128,512]{2,1,0:T(8,128)(2,1)S(1)} %get-tuple-element.94), channel_id=1, source_target_pairs={{0,1},{1,2},{2,3},{3,4},{4,5},{5,6},{6,7},{8,9},{9,10},{10,11},{11... | collective-permute-start | bytes 393224 | tf_op jit(solution)/shard_map/ppermute | solution.py:502
  329.0 6.9 collective-permute-start.9
  453.0 252.3 %all-reduce.11.cloned.1.call-start = ((), (), s32[]{:S(2)}) async-start(), calls=%async_computation.1 | async-start | bytes 3670016 | tf_op jit(solution)/shard_map/psum | solution.py:588
  453.6 53.4 %copy-start.1 = (bf16[3,576,512]{2,1,0:T(8,128)(2,1)S(1)}, bf16[3,576,512]{2,1,0:T(8,128)(2,1)}, u32[]{:S(2)}) copy-start(bf16[3,576,512]{2,1,0:T(8,128)(2,1)} %shard_map.238) | copy-start | bytes 5308420
  501.3 24.0 %collective-permute-start.10 = (bf16[1,128,512]{2,1,0:T(8,128)(2,1)S(1)}, bf16[1,128,512]{2,1,0:T(8,128)(2,1)S(1)}, u32[]{:S(2)}, u32[]{:S(2)}) collective-permute-start(bf16[1,128,512]{2,1,0:T(8,128)(2,1)S(1)} %get-tuple-element.92), channel_id=1, source_target_pairs={{0,1},{1,2},{2,3},{3,4},{4,5},{5,6},{6,7},{8,9},{9,10},{10,11},{11... | collective-permute-start | bytes 393224 | tf_op jit(solution)/shard_map/ppermute | solution.py:502
  505.5 19.8 %collective-permute-start.11 = (bf16[1,128,512]{2,1,0:T(8,128)(2,1)S(1)}, bf16[1,128,512]{2,1,0:T(8,128)(2,1)S(1)}, u32[]{:S(2)}, u32[]{:S(2)}) collective-permute-start(bf16[1,128,512]{2,1,0:T(8,128)(2,1)S(1)} %get-tuple-element.93), channel_id=1, source_target_pairs={{1,0},{2,1},{3,2},{4,3},{5,4},{6,5},{7,6},{9,8},{10,9},{11,10},{12... | collective-permute-start | bytes 393224 | tf_op jit(solution)/shard_map/ppermute | solution.py:505
  623.1 80.6 %copy-start.30 = (f32[28672]{0:T(1024)S(1)}, f32[28672]{0:T(1024)}, u32[]{:S(2)}) copy-start(f32[28672]{0:T(1024)} %param.17) | copy-start | bytes 344068
  623.1 80.6 %copy-start.31 = (f32[28672]{0:T(1024)S(1)}, f32[28672]{0:T(1024)}, u32[]{:S(2)}) copy-start(f32[28672]{0:T(1024)} %param.22) | copy-start | bytes 344068
  623.1 80.6 %copy-start.32 = (f32[28672]{0:T(1024)S(1)}, f32[28672]{0:T(1024)}, u32[]{:S(2)}) copy-start(f32[28672]{0:T(1024)} %param.21) | copy-start | bytes 344068
  (40 other events, 325.5 us)
Sparse Core Ops, SparseCore 0:
  16.4 70.3 all-gather.1
  453.1 169.9 all-reduce.12
  626.0 47.1 all-reduce.10
